TPU v7x, 32 devices: a whole 2x2x4 slice. The times are simulated.
32 devices in a mesh: grp: 2 (over y), sta: 4 (over z), hr: 2 (over x), sub: 2 (over core).
Axes of the slice: x: 2, y: 2, z: 4, core: 2. Of those that a mesh axis runs over, the one named last changes fastest.
Arguments:
- spectra: bfloat16 [4, 1000, 2, 4096], P(('grp', 'hr'), 'sub', None, 'sta'), parts along dimension 0, may hold values from -400 to 400
- pair_blocks: int32 [4, 2], replicated, may hold values from 0 to 31, as said below
- pair_owner: int32 [4], replicated, may hold values from 0 to 3, as said below
- block_members: int32 [32, 128], P('sta'), may hold values from 0 to 1023, as said below
Outputs:
- correlations: bfloat16 [32, 12, 128, 128], P(('grp', 'hr', 'sub'), 'sta'), parts along dimension 0
There are 2 independent parts, one for each index of `grp`. A program takes and returns all parts, laid end to end along the dimension named above; an argument that names none is the same for every part. Nothing has to cross between parts.
Inputs may be any that keep to these rules, and one draw needn't show every extreme that they name: `pair_blocks`: each row names two different blocks; block g holds stations of index g // 8 of sta. The blocks of the pairs of owner o lie on indices o, o + 1, o + 2 or o + 3 (mod 4) of sta, and the distinct blocks named by the pairs of one owner lie on distinct indices of sta. `pair_owner`: at most 3 pairs share an owner, and some owner has exactly 3. `block_members`: the 8 rows of the blocks of one index of sta hold each of 0 to 1023 once.
All inputs are finite; a program needn't handle non-finite values.
Results may differ from a plain program's by a relative error of at most 0.0063.
Values may be sent and summed in bfloat16 or wider, within the bound.
No kernel may reach another device: no remote copies, remote signals or barrier semaphores. Data moves between devices by JAX's collectives and lax.ppermute only.
A program may use at most 64 MiB of HBM per device.

v0:
```python
import math

import jax
import jax.numpy as jnp
from jax import lax
from jax.sharding import PartitionSpec as P

F = 1000
BAND = 50
LAGS = 16
CAP = 3


EPSILON = 1e-05


def whiten(spectra):
    values = spectra.astype(jnp.float32)
    hour_count, freq_count, part_count, station_count = values.shape
    banded = values.reshape(hour_count, freq_count // BAND, BAND, part_count, station_count)
    band_power = jnp.mean(banded * banded, axis=(2, 3), keepdims=True)
    whitened = banded / jnp.sqrt(band_power + EPSILON)
    return whitened.reshape(hour_count, freq_count, part_count, station_count).astype(jnp.bfloat16)


def lag_phases(freq_ids, lag_shift):
    angle_turns = jnp.mod(freq_ids * lag_shift, F).astype(jnp.float32) * (2.0 * math.pi / F)
    return (jnp.cos(angle_turns), jnp.sin(angle_turns))


def rotate(block, cosine, sine_part):
    real_part = block[..., 0, :].astype(jnp.float32)
    imag_part = block[..., 1, :].astype(jnp.float32)
    cos_col = cosine[:, None]
    sin_col = sine_part[:, None]
    turned = jnp.stack(
        [real_part * cos_col - imag_part * sin_col, real_part * sin_col + imag_part * cos_col],
        axis=-2,
    )
    return turned.astype(jnp.bfloat16)


def lag_block(left_slots, right_slots, first_freq, norming):
    slot_count, hour_count, freq_count, part_count, width = left_slots.shape
    freq_ids = first_freq + jnp.arange(freq_count, dtype=jnp.int32)

    def lag_term(begin_row, row_count):

        def one_lag(lag_row):
            cosine, sine_part = lag_phases(freq_ids, lag_row - LAGS // 2)
            turned = rotate(left_slots, cosine, sine_part).reshape(slot_count, -1, width)
            return (
                jnp.einsum("ski,skj->sij", turned, right_slots, preferred_element_type=jnp.float32)
                * norming
            )

        return lax.map(one_lag, jnp.arange(row_count, dtype=jnp.int32))

    return lag_term


def on_device(spectra, pair_blocks, pair_owner, block_members):
    hour_count, sub_freqs, part_count, station_count = spectra.shape
    block_count, width = block_members.shape
    sta_count = lax.axis_size("sta")
    my_sta = lax.axis_index("sta")
    sub_index = lax.axis_index("sub")
    norming = 1.0 / math.sqrt(hour_count * lax.axis_size("hr") * F)
    lag_rows = LAGS // (lax.axis_size("hr") * lax.axis_size("sub"))
    first_freq = sub_index * sub_freqs
    whitened = whiten(spectra)
    picked = jnp.take(whitened, block_members.reshape(-1), axis=3)
    blocks = jnp.transpose(
        picked.reshape(hour_count, sub_freqs, part_count, block_count, width), (3, 0, 1, 2, 4)
    ).reshape(block_count, -1, width)
    pair_total = pair_owner.shape[0]
    pair_ids = jnp.arange(pair_total, dtype=jnp.int32)
    earlier = pair_ids[:, None] > pair_ids[None, :]
    same_owner = pair_owner[:, None] == pair_owner[None, :]
    owner_rank = jnp.sum((earlier & same_owner).astype(jnp.int32), axis=1)
    slot_match = (pair_owner[None, :] == my_sta) & (
        owner_rank[None, :] == jnp.arange(CAP, dtype=jnp.int32)[:, None]
    )
    filled = jnp.any(slot_match, axis=1)
    slot_pair = jnp.sum(jnp.where(slot_match, pair_ids[None, :], 0), axis=1)
    zero_value = jnp.zeros((), jnp.bfloat16)
    my_blocks = my_sta * block_count + jnp.arange(block_count, dtype=jnp.int32)
    named_here = (pair_blocks[:, 0:1] == my_blocks[None, :]) | (
        pair_blocks[:, 1:2] == my_blocks[None, :]
    )
    owner_hit = pair_owner[:, None] == jnp.arange(sta_count, dtype=jnp.int32)[None, :]
    wanted = jnp.any(owner_hit[:, :, None] & named_here[:, None, :], axis=0)
    chosen = jnp.sum(
        jnp.where(wanted, jnp.arange(block_count, dtype=jnp.int32)[None, :], 0), axis=1
    )
    has_block = jnp.any(wanted, axis=1)
    left_home = pair_blocks[slot_pair, 0] // block_count
    right_home = pair_blocks[slot_pair, 1] // block_count
    outgoing = jnp.where(has_block[:, None, None], blocks[chosen], zero_value)
    incoming = lax.all_to_all(outgoing, "sta", split_axis=0, concat_axis=0, tiled=True)
    left_source = incoming[left_home]
    right_source = incoming[right_home]
    slot_used = filled[:, None, None]
    left_slots = jnp.where(slot_used, left_source, zero_value)
    right_slots = jnp.where(slot_used, right_source, zero_value)
    lag_term = lag_block(
        left_slots.reshape(CAP, hour_count, sub_freqs, part_count, width),
        right_slots,
        first_freq,
        norming,
    )
    summed = lax.psum_scatter(
        lag_term(jnp.int32(0), lag_rows * lax.axis_size(("hr", "sub"))),
        ("hr", "sub"),
        scatter_dimension=0,
        tiled=True,
    )
    result = summed.astype(jnp.bfloat16)
    return result


def solution(mesh):
    placed = (P(("grp", "hr"), "sub", None, "sta"), P(), P(), P("sta", None))
    return jax.shard_map(
        on_device,
        mesh=mesh,
        in_specs=placed,
        out_specs=P(("grp", "hr", "sub"), "sta", None, None),
        check_vma=False,
    )
```

profile of v0, /device:TPU:0, one launch (start us, length us, event | category | flops | bytes accessed | tf_op | source)
XLA Modules:
  0.0 258.4 jit_solution(5684713539665393006)
XLA Ops:
  8.4 8.3 %copy.17 = bf16[1,500,2,1024]{1,2,3,0:T(2,128)(2,1)S(1)} copy(bf16[1,500,2,1024]{3,2,1,0:T(2,128)(2,1)} %param.6) | data formatting | bytes 4096000 | tf_op args[0]
  16.7 7.3 %fusion.12 = f32[500,1024]{0,1:T(8,128)} fusion(bf16[1,500,2,1024]{1,2,3,0:T(2,128)(2,1)S(1)} %copy.17), kind=kLoop, calls=%fused_computation.25 | loop fusion | flops 2560000 | bytes 4096000 | tf_op jit(solution)/shard_map/reduce_sum | solution.py:21
  24.0 2.9 %copy.18 = f32[500,1024]{1,0:T(8,128)} copy(f32[500,1024]{0,1:T(8,128)} %fusion.12) | data formatting | bytes 4096000 | tf_op jit(solution)/shard_map/reduce_sum | solution.py:21
  26.9 3.0 %reduce_sum.49 = f32[10,50,1024]{2,1,0:T(8,128)} reshape(f32[500,1024]{1,0:T(8,128)} %copy.18) | data formatting | bytes 4096000 | tf_op jit(solution)/shard_map/reduce_sum | solution.py:21
  33.6 3.0 %div.45 = f32[500,1024]{1,0:T(8,128)} reshape(f32[10,50,1024]{2,1,0:T(8,128)} %div.44) | data formatting | bytes 4096000 | tf_op jit(solution)/shard_map/div | solution.py:22
  36.6 2.9 %copy.19 = f32[500,1024]{0,1:T(8,128)} copy(f32[500,1024]{1,0:T(8,128)} %div.45) | data formatting | bytes 4096000 | tf_op jit(solution)/shard_map/div | solution.py:22
  39.6 4.8 %fusion.15 = bf16[500,2,1024]{0,1,2:T(2,128)(2,1)} fusion(bf16[1,500,2,1024]{1,2,3,0:T(2,128)(2,1)S(1)} %copy.17, f32[500,1024]{0,1:T(8,128)} %copy.19), kind=kLoop, calls=%fused_computation.29 | loop fusion | flops 3072000 | bytes 6144000 | tf_op jit(solution)/shard_map/convert_element_type | solution.py:23
  44.4 12.6 %gather_fusion = bf16[1024,500,2]{1,2,0:T(2,128)(2,1)} fusion(bf16[500,2,1024]{0,1,2:T(2,128)(2,1)} %fusion.15, s32[1024]{0:T(1024)S(1)} %broadcast_clamp_fusion), kind=kCustom, calls=%fused_computation | custom fusion | bytes 4100096 | tf_op jit(solution)/shard_map/jit(_take)/gather | solution.py:72
  57.0 3.9 %fusion.14 = bf16[8,1,500,2,128]{2,3,4,0,1:T(2,128)(2,1)S(1)} fusion(bf16[1,500,2,8,128]{1,2,4,3,0:T(2,128)(2,1)} %bitcast.72, pred[8,128]{1,0:T(8,128)(4,1)S(1)} %compare_and_fusion), kind=kLoop, calls=%fused_computation.28 | loop fusion | flops 1024000 | bytes 4097024 | tf_op jit(solution)/shard_map/transpose | solution.py:73
  61.0 6.4 %copy.20 = bf16[8,1,500,2,128]{4,3,2,0,1:T(2,128)(2,1)} copy(bf16[8,1,500,2,128]{2,3,4,0,1:T(2,128)(2,1)S(1)} %fusion.14) | data formatting | bytes 4096000 | tf_op jit(solution)/shard_map/transpose | solution.py:73
  70.8 6.3 %all-to-all-start = ((bf16[4,1000,128]{2,1,0:T(8,128)(2,1)}), bf16[4,1000,128]{2,1,0:T(8,128)(2,1)S(1)}, u32[]{:S(2)}, u32[]{:S(2)}) async-start(bf16[4,1000,128]{2,1,0:T(8,128)(2,1)} %broadcast_select_fusion.2), calls=%async_computation | async-start | bytes 2048000 | tf_op jit(solution)/shard_map/all_to_all | solution.py:100
  79.0 23.4 %all-to-all-done = bf16[4,1000,128]{2,1,0:T(8,128)(2,1)S(1)} async-done(((bf16[4,1000,128]{2,1,0:T(8,128)(2,1)}), bf16[4,1000,128]{2,1,0:T(8,128)(2,1)S(1)}, u32[]{:S(2)}, u32[]{:S(2)}) %all-to-all-start) | async-done | bytes 1024032 | tf_op jit(solution)/shard_map/all_to_all | solution.py:100
  104.7 107.7 %while.13 = (s32[]{:T(128)}, f32[16,3,128,128]{3,2,1,0:T(8,128)}, bf16[3,1,500,2,128]{4,3,2,0,1:T(2,128)(2,1)S(1)}, s32[16]{0:T(128)S(1)}, bf16[3,1000,128]{2,1,...) while((s32[]{:T(128)}, f32[16,3,128,128]{3,2,1,0:T(8,128)}, ...), condition=%wide.region_9.10_spmd.clone, body=%wide.region_8.9_spmd.clone.sunk | while | flops 101814152 | bytes 4813237 | solution.py:57
  105.9 2.7 %subtract_convert_fusion.2 = (bf16[3,1,500,1,128]{4,3,2,0,1:T(2,128)(2,1)S(1)}, bf16[3,1,500,1,128]{4,3,2,0,1:T(2,128)(2,1)S(1)}) fusion(bf16[3,1,500,2,128]{4,3,2,0,1:T(2,128)(2,1)S(1)} %get-tuple-element.185, f32[500]{0:T(512)S(1)} %get-tuple-element.163, f32[500]{0:T(512)S(1)} %get-tuple-element.164), kind=kLoop, calls=%fused_computation.12.clone.1 | loop fusion | flops 1920000 | bytes 1540000 | tf_op jit(solution)/shard_map/convert
  112.6 2.7 %subtract_convert_fusion.2 = (bf16[3,1,500,1,128]{4,3,2,0,1:T(2,128)(2,1)S(1)}, bf16[3,1,500,1,128]{4,3,2,0,1:T(2,128)(2,1)S(1)}) fusion(bf16[3,1,500,2,128]{4,3,2,0,1:T(2,128)(2,1)S(1)} %get-tuple-element.185, f32[500]{0:T(512)S(1)} %get-tuple-element.163, f32[500]{0:T(512)S(1)} %get-tuple-element.164), kind=kLoop, calls=%fused_computation.12.clone.1 | loop fusion | flops 1920000 | bytes 1540000 | tf_op jit(solution)/shard_map/convert
  119.3 2.7 %subtract_convert_fusion.2 = (bf16[3,1,500,1,128]{4,3,2,0,1:T(2,128)(2,1)S(1)}, bf16[3,1,500,1,128]{4,3,2,0,1:T(2,128)(2,1)S(1)}) fusion(bf16[3,1,500,2,128]{4,3,2,0,1:T(2,128)(2,1)S(1)} %get-tuple-element.185, f32[500]{0:T(512)S(1)} %get-tuple-element.163, f32[500]{0:T(512)S(1)} %get-tuple-element.164), kind=kLoop, calls=%fused_computation.12.clone.1 | loop fusion | flops 1920000 | bytes 1540000 | tf_op jit(solution)/shard_map/convert
  126.0 2.7 %subtract_convert_fusion.2 = (bf16[3,1,500,1,128]{4,3,2,0,1:T(2,128)(2,1)S(1)}, bf16[3,1,500,1,128]{4,3,2,0,1:T(2,128)(2,1)S(1)}) fusion(bf16[3,1,500,2,128]{4,3,2,0,1:T(2,128)(2,1)S(1)} %get-tuple-element.185, f32[500]{0:T(512)S(1)} %get-tuple-element.163, f32[500]{0:T(512)S(1)} %get-tuple-element.164), kind=kLoop, calls=%fused_computation.12.clone.1 | loop fusion | flops 1920000 | bytes 1540000 | tf_op jit(solution)/shard_map/convert
  132.8 2.7 %subtract_convert_fusion.2 = (bf16[3,1,500,1,128]{4,3,2,0,1:T(2,128)(2,1)S(1)}, bf16[3,1,500,1,128]{4,3,2,0,1:T(2,128)(2,1)S(1)}) fusion(bf16[3,1,500,2,128]{4,3,2,0,1:T(2,128)(2,1)S(1)} %get-tuple-element.185, f32[500]{0:T(512)S(1)} %get-tuple-element.163, f32[500]{0:T(512)S(1)} %get-tuple-element.164), kind=kLoop, calls=%fused_computation.12.clone.1 | loop fusion | flops 1920000 | bytes 1540000 | tf_op jit(solution)/shard_map/convert
  139.5 2.7 %subtract_convert_fusion.2 = (bf16[3,1,500,1,128]{4,3,2,0,1:T(2,128)(2,1)S(1)}, bf16[3,1,500,1,128]{4,3,2,0,1:T(2,128)(2,1)S(1)}) fusion(bf16[3,1,500,2,128]{4,3,2,0,1:T(2,128)(2,1)S(1)} %get-tuple-element.185, f32[500]{0:T(512)S(1)} %get-tuple-element.163, f32[500]{0:T(512)S(1)} %get-tuple-element.164), kind=kLoop, calls=%fused_computation.12.clone.1 | loop fusion | flops 1920000 | bytes 1540000 | tf_op jit(solution)/shard_map/convert
  146.2 2.7 %subtract_convert_fusion.2 = (bf16[3,1,500,1,128]{4,3,2,0,1:T(2,128)(2,1)S(1)}, bf16[3,1,500,1,128]{4,3,2,0,1:T(2,128)(2,1)S(1)}) fusion(bf16[3,1,500,2,128]{4,3,2,0,1:T(2,128)(2,1)S(1)} %get-tuple-element.185, f32[500]{0:T(512)S(1)} %get-tuple-element.163, f32[500]{0:T(512)S(1)} %get-tuple-element.164), kind=kLoop, calls=%fused_computation.12.clone.1 | loop fusion | flops 1920000 | bytes 1540000 | tf_op jit(solution)/shard_map/convert
  153.0 2.7 %subtract_convert_fusion.2 = (bf16[3,1,500,1,128]{4,3,2,0,1:T(2,128)(2,1)S(1)}, bf16[3,1,500,1,128]{4,3,2,0,1:T(2,128)(2,1)S(1)}) fusion(bf16[3,1,500,2,128]{4,3,2,0,1:T(2,128)(2,1)S(1)} %get-tuple-element.185, f32[500]{0:T(512)S(1)} %get-tuple-element.163, f32[500]{0:T(512)S(1)} %get-tuple-element.164), kind=kLoop, calls=%fused_computation.12.clone.1 | loop fusion | flops 1920000 | bytes 1540000 | tf_op jit(solution)/shard_map/convert
  166.4 2.7 %subtract_convert_fusion.2 = (bf16[3,1,500,1,128]{4,3,2,0,1:T(2,128)(2,1)S(1)}, bf16[3,1,500,1,128]{4,3,2,0,1:T(2,128)(2,1)S(1)}) fusion(bf16[3,1,500,2,128]{4,3,2,0,1:T(2,128)(2,1)S(1)} %get-tuple-element.185, f32[500]{0:T(512)S(1)} %get-tuple-element.163, f32[500]{0:T(512)S(1)} %get-tuple-element.164), kind=kLoop, calls=%fused_computation.12.clone.1 | loop fusion | flops 1920000 | bytes 1540000 | tf_op jit(solution)/shard_map/convert
  173.1 2.7 %subtract_convert_fusion.2 = (bf16[3,1,500,1,128]{4,3,2,0,1:T(2,128)(2,1)S(1)}, bf16[3,1,500,1,128]{4,3,2,0,1:T(2,128)(2,1)S(1)}) fusion(bf16[3,1,500,2,128]{4,3,2,0,1:T(2,128)(2,1)S(1)} %get-tuple-element.185, f32[500]{0:T(512)S(1)} %get-tuple-element.163, f32[500]{0:T(512)S(1)} %get-tuple-element.164), kind=kLoop, calls=%fused_computation.12.clone.1 | loop fusion | flops 1920000 | bytes 1540000 | tf_op jit(solution)/shard_map/convert
  212.4 37.2 %reduce-scatter.2.cloned.1.call-done = f32[4,3,128,128]{3,2,1,0:T(8,128)} async-done(((f32[16,3,128,128]{3,2,1,0:T(8,128)}), f32[4,3,128,128]{3,2,1,0:T(8,128)}) %reduce-scatter.2.cloned.1.call-update) | async-done | bytes 786448 | tf_op jit(solution)/shard_map/reduce_scatter | solution.py:112
  (112 shorter events, 87.0 us)
Async XLA Ops:
  39.6 4.8 %copy-start.1 = (s32[8,128]{1,0:T(8,128)S(1)}, s32[8,128]{1,0:T(8,128)}, u32[]{:S(2)}) copy-start(s32[8,128]{1,0:T(8,128)} %param.9) | copy-start | bytes 12292
  69.7 7.5 %copy-start.2 = (s32[4]{0:T(128)S(1)}, s32[4]{0:T(128)}, u32[]{:S(2)}) copy-start(s32[4]{0:T(128)} %param.8) | copy-start | bytes 52
  69.7 7.8 %copy-start = (s32[4,2]{0,1:T(2,128)S(1)}, s32[4,2]{0,1:T(2,128)}, u32[]{:S(2)}) copy-start(s32[4,2]{0,1:T(2,128)} %param.7) | copy-start | bytes 100
  70.8 31.5 %all-to-all-start = ((bf16[4,1000,128]{2,1,0:T(8,128)(2,1)}), bf16[4,1000,128]{2,1,0:T(8,128)(2,1)S(1)}, u32[]{:S(2)}, u32[]{:S(2)}) async-start(bf16[4,1000,128]{2,1,0:T(8,128)(2,1)} %broadcast_select_fusion.2), calls=%async_computation | async-start | bytes 2048000 | tf_op jit(solution)/shard_map/all_to_all | solution.py:100
  77.2 172.5 %reduce-scatter.2.cloned.1.call-start = ((), (), s32[]{:S(2)}) async-start(), calls=%async_computation.2 | async-start | bytes 3932160 | tf_op jit(solution)/shard_map/reduce_scatter | solution.py:112
Sparse Core Ops, SparseCore 0:
  212.5 37.0 reduce-scatter.1
where the time goes:
time: 259 us; the launch traced here: 258 us
  other arithmetic  95 us (37%)
  waiting for transfers between devices  60.6 us (23%)
  local copies, waits for them, and re-layouts  55.5 us (21%)
  matrix products  18.4 us (7%)
  between operations  13.5 us (5%)
  loops' own time  9.07 us (4%)
  starting transfers between devices  6.32 us (2%)
    another operation x16, other arithmetic  42.6 us
    reduce_scatter x1, waiting for transfers between devices, on_device(): lax.psum_scatter(lag_term(jnp.int32(0), lag_rows * lax.axis_size(('hr', '...  37.2 us
    another operation x16, other arithmetic, rotate(): jnp.stack([real_part * cos_col - imag_part * sin_col, real_part * sin_col...  27.9 us
    all_to_all x1, waiting for transfers between devices, on_device(): lax.all_to_all(outgoing, 'sta', split_axis=0, concat_axis=0, tiled=True)  23.4 us
    dot_general x16, matrix products, one_lag(): jnp.einsum('ski,skj->sij', turned, right_slots, preferred_element_type=jn...  18.4 us
    gather x1, local copies, waits for them, and re-layouts, on_device(): picked = jnp.take(whitened, block_members.reshape(-1), axis=3)  12.6 us
    reduce_sum x2, other arithmetic, whiten(): band_power = jnp.mean(banded * banded, axis=(2, 3), keepdims=True)  9.21 us
    another operation x1, loops' own time, lag_term(): return lax.map(one_lag, jnp.arange(row_count, dtype=jnp.int32))  9.07 us
  transfers between devices with their start and end apart: 2, of which 2 were waited for; matrix products, arithmetic and copies ran while one was open for 1% of the time, Pallas kernels for 0%

commit v1 on v0

v1 whole, which is shorter than its diff:
```python
import functools
import math

import jax
import jax.numpy as jnp
import numpy as np
from jax import lax
from jax.experimental import pallas as pl
from jax.experimental.pallas import tpu as pltpu
from jax.sharding import PartitionSpec as P

BAND = 50
LAGS = 16
CAP = 3
REACH = 4
EPSILON = 1e-05
LANES = 128
F32 = jnp.float32
BF16 = jnp.bfloat16
VMEM_LIMIT = 48 * 1024 * 1024

NT = (((1,), (1,)), ((), ()))


def dot_nt(left, right):
    return lax.dot_general(left, right, NT, preferred_element_type=F32)


def iota(shape, dim):
    return lax.broadcasted_iota(jnp.int32, shape, dim)


def band_matrix(chunk, freqs):
    row, col = iota((2 * LANES, LANES), 0), iota((2 * LANES, LANES), 1)
    freq = chunk * LANES + row % LANES
    low = (col % 16) * BAND
    hit = (freq >= low) & (freq < low + BAND) & (freq < freqs) & (col < 48)
    return jnp.where(hit, 1.0, 0.0).astype(BF16)


def pick_kernel(sta_axis, pair_ref, owner_ref, member_ref, x_ref, *rest):
    outs, (x_buf, y_buf, z_buf, sems) = rest[:REACH], rest[REACH:]
    tiles, freqs = x_buf.shape[0], x_buf.shape[1]
    block_count, width = member_ref.shape
    chunks = y_buf.shape[1] // (2 * LANES)

    def fetch(tile):
        return pltpu.make_async_copy(
            x_ref.at[0, :, :, pl.ds(tile * LANES, LANES)], x_buf.at[tile], sems.at[tile]
        )

    for tile in range(tiles):
        fetch(tile).start()

    my_sta = lax.axis_index(sta_axis)
    sta_count = lax.axis_size(sta_axis)
    members = jnp.transpose(member_ref[...].astype(F32))
    block_col = iota(members.shape, 1)
    station = []
    for reach in range(REACH):
        owner = lax.rem(my_sta - reach + REACH * sta_count, sta_count)
        chosen = jnp.int32(0)
        for pair in range(owner_ref.shape[0]):
            for side in range(2):
                block = pair_ref[side, pair]
                hit = (owner_ref[pair] == owner) & (block // block_count == my_sta)
                chosen = jnp.where(hit, lax.rem(block, block_count), chosen)
        picked = jnp.where(block_col == chosen, members, 0.0)
        station.append(jnp.sum(picked, axis=1, keepdims=True).astype(jnp.int32))
    station = jnp.concatenate(station, axis=0)

    lane = iota((REACH * width, LANES), 1)

    def one_hot(tile):
        return jnp.where(station == lane + tile * LANES, 1.0, 0.0).astype(BF16)

    half = tiles // 2
    y_buf[...] = jnp.zeros_like(y_buf)
    total = None
    for first in (0, half):
        span = range(first, first + half)
        hot = jnp.concatenate([one_hot(tile) for tile in span], axis=1)
        for tile in span:
            fetch(tile).wait()
        x = jnp.concatenate(
            [x_buf.at[tile].reshape(2 * freqs, LANES)[...] for tile in span], axis=1
        )
        part = dot_nt(hot, x)
        total = part if total is None else total + part
    y_buf[:, : 2 * freqs] = total.astype(BF16)

    row, col = iota((2 * LANES, 2 * LANES), 0), iota((2 * LANES, 2 * LANES), 1)
    split = jnp.where(row == 2 * (col % LANES) + col // LANES, 1.0, 0.0).astype(BF16)
    power = None
    for chunk in range(chunks):
        z = jnp.dot(
            y_buf[:, chunk * 2 * LANES : (chunk + 1) * 2 * LANES],
            split,
            preferred_element_type=F32,
        )
        z_buf[chunk] = z
        square = z * z
        high = square.astype(BF16)
        low = (square - high.astype(F32)).astype(BF16)
        bands = band_matrix(chunk, freqs)
        part = jnp.dot(high, bands, preferred_element_type=F32) + jnp.dot(
            low, bands, preferred_element_type=F32
        )
        power = part if power is None else power + part
    scale = lax.rsqrt(power * (1.0 / (2 * BAND)) + EPSILON)
    high = scale.astype(BF16)
    rest1 = scale - high.astype(F32)
    mid = rest1.astype(BF16)
    low = rest1 - mid.astype(F32)
    third = iota(scale.shape, 1) // 16
    pieces = jnp.where(
        third == 0, high.astype(F32), jnp.where(third == 1, mid.astype(F32), low)
    ).astype(BF16)
    for chunk in range(chunks):
        white = (z_buf[chunk] * dot_nt(pieces, band_matrix(chunk, freqs))).astype(BF16)
        for reach in range(REACH):
            rows = slice(reach * width, (reach + 1) * width)
            outs[reach][:, chunk * LANES : (chunk + 1) * LANES] = white[rows, :LANES]
            outs[reach][:, (chunks + chunk) * LANES : (chunks + chunk + 1) * LANES] = white[
                rows, LANES:
            ]


def pick_blocks(spectra, pair_sides, pair_owner, block_members):
    _, freqs, parts, stations = spectra.shape
    block_count, width = block_members.shape
    tiles = stations // LANES
    chunks = -(-freqs // LANES)
    rows = REACH * width
    smem = pl.BlockSpec(memory_space=pltpu.SMEM)
    vmem = pl.BlockSpec(memory_space=pltpu.VMEM)
    return pl.pallas_call(
        functools.partial(pick_kernel, "sta"),
        out_shape=[jax.ShapeDtypeStruct((width, chunks * 2 * LANES), BF16)] * REACH,
        in_specs=[smem, smem, vmem, pl.BlockSpec(memory_space=pltpu.HBM)],
        out_specs=[vmem] * REACH,
        scratch_shapes=[
            pltpu.VMEM((tiles, freqs, parts, LANES), BF16),
            pltpu.VMEM((rows, chunks * 2 * LANES), BF16),
            pltpu.VMEM((chunks, rows, 2 * LANES), F32),
            pltpu.SemaphoreType.DMA((tiles,)),
        ],
        compiler_params=pltpu.CompilerParams(vmem_limit_bytes=VMEM_LIMIT),
        cost_estimate=pl.CostEstimate(
            flops=2 * rows * stations * freqs * parts,
            bytes_accessed=2 * spectra.size + 4 * rows * chunks * LANES,
            transcendentals=0,
        ),
        name="pick_and_whiten",
    )(pair_sides, pair_owner, block_members, spectra)


def phase_table(sub_count, sub_freqs, groups, lag_rows):
    chunks = -(-sub_freqs // LANES)
    freq = np.arange(sub_count * sub_freqs, dtype=np.int64).reshape(sub_count, 1, sub_freqs)
    total = sub_count * sub_freqs
    middle = [2 * (group * lag_rows - LAGS // 2) + lag_rows - 1 for group in range(groups)]
    away = [step for step in range(1, lag_rows) if step % 2 != lag_rows % 2]
    twice = np.array(middle + away, dtype=np.int64).reshape(1, -1, 1)
    angle = np.mod(freq * twice, 2 * total) * (math.pi / total)
    table = np.stack([np.cos(angle), np.sin(angle)], axis=2)
    table = table.reshape(sub_count, -1, sub_freqs)
    pad = ((0, 0), (0, -table.shape[1] % 8), (0, chunks * LANES - sub_freqs))
    return np.pad(table, pad).astype(np.float32), len(away)


def lag_kernel(hops, lag_rows, away, block_count, pair_ref, owner_ref, table_ref, *rest):
    sub_count = lax.axis_size("sub")
    hr_count = lax.axis_size("hr")
    blocks = rest[: REACH * sub_count]
    outs = rest[REACH * sub_count : REACH * sub_count + len(hops)]
    left_buf, right_buf, turned_buf, versions = rest[REACH * sub_count + len(hops) :]
    width = left_buf.shape[1]
    span = left_buf.shape[2] // 2
    middle_lag = lag_rows % 2
    my_sta = lax.axis_index("sta")
    my_sub = lax.axis_index("sub")
    my_hr = lax.axis_index("hr")
    sta_count = lax.axis_size("sta")
    pair_count = owner_ref.shape[0]
    groups = hr_count * sub_count

    for slot in range(CAP):
        count = jnp.int32(0)
        left, right = jnp.int32(-1), jnp.int32(-1)
        for pair in range(pair_count):
            mine = owner_ref[pair] == my_sta
            hit = mine & (count == slot)
            ends = [
                lax.rem(pair_ref[side, pair] // block_count - my_sta + sta_count, sta_count)
                for side in range(2)
            ]
            left = jnp.where(hit, ends[0], left)
            right = jnp.where(hit, ends[1], right)
            count = count + mine.astype(jnp.int32)

        @pl.when(left < 0)
        def _():
            for out in outs:
                out[:, slot] = jnp.zeros((lag_rows, width, width), out.dtype)

        for reach in range(REACH):

            @pl.when(left == reach)
            def _():
                for step in range(sub_count):
                    left_buf[step] = blocks[reach * sub_count + step][...]

            @pl.when(right == reach)
            def _():
                for step in range(sub_count):
                    right_buf[step] = blocks[reach * sub_count + step][...]

        @pl.when(left >= 0)
        def _():
            for step in range(sub_count):
                sub = lax.rem(my_sub + step, sub_count)
                base = step * 2 * span
                real = right_buf[step, :, :span].astype(F32)
                imag = right_buf[step, :, span:].astype(F32)
                if middle_lag:
                    versions[:width, base : base + 2 * span] = right_buf[step]
                for index in range(away):
                    row = 2 * (groups + index)
                    cosine = table_ref[sub, row : row + 1, :]
                    sine = table_ref[sub, row + 1 : row + 2, :]
                    top = (middle_lag + 2 * index) * width
                    versions[top : top + width, base : base + span] = (real * cosine).astype(BF16)
                    versions[top : top + width, base + span : base + 2 * span] = (
                        imag * cosine
                    ).astype(BF16)
                    top += width
                    versions[top : top + width, base : base + span] = (imag * sine).astype(BF16)
                    versions[top : top + width, base + span : base + 2 * span] = (
                        -(real * sine)
                    ).astype(BF16)
            for out, hop in zip(outs, hops):
                group = lax.rem(my_hr + hop, hr_count) * sub_count + my_sub
                for step in range(sub_count):
                    sub = lax.rem(my_sub + step, sub_count)
                    base = step * 2 * span
                    real = left_buf[step, :, :span].astype(F32)
                    imag = left_buf[step, :, span:].astype(F32)
                    cosine = table_ref[sub, pl.ds(2 * group, 1), :]
                    sine = table_ref[sub, pl.ds(2 * group + 1, 1), :]
                    turned_buf[:, base : base + span] = (real * cosine - imag * sine).astype(BF16)
                    turned_buf[:, base + span : base + 2 * span] = (
                        real * sine + imag * cosine
                    ).astype(BF16)
                product = dot_nt(turned_buf[...], versions[...])
                if middle_lag:
                    out[lag_rows // 2, slot] = product[:, :width].astype(out.dtype)
                for index in range(away):
                    start = (middle_lag + 2 * index) * width
                    even = product[:, start : start + width]
                    odd = product[:, start + width : start + 2 * width]
                    below = (lag_rows - 1) // 2 - index - middle_lag
                    above = lag_rows - 1 - below
                    out[above, slot] = (even + odd).astype(out.dtype)
                    out[below, slot] = (even - odd).astype(out.dtype)


def on_device(spectra, pair_blocks, pair_owner, block_members):
    hour_count, sub_freqs, _, _ = spectra.shape
    block_count, width = block_members.shape
    sta_count, hr_count, sub_count = (lax.axis_size(axis) for axis in ("sta", "hr", "sub"))
    groups = hr_count * sub_count
    lag_rows = LAGS // groups
    norming = 1.0 / math.sqrt(hour_count * hr_count * sub_count * sub_freqs)
    pair_sides = pair_blocks.T
    table, away = phase_table(sub_count, sub_freqs, groups, lag_rows)
    table = jnp.asarray(table)

    picked = pick_blocks(spectra, pair_sides, pair_owner, block_members)
    arrived = [picked[0]]
    for reach in range(1, REACH):
        to_owner = [(home, (home - reach) % sta_count) for home in range(sta_count)]
        arrived.append(lax.ppermute(picked[reach], "sta", to_owner))
    blocks = []
    for block in arrived:
        blocks.append(block)
        for step in range(1, sub_count):
            swap = [((sub + step) % sub_count, sub) for sub in range(sub_count)]
            blocks.append(lax.ppermute(block, "sub", swap))

    smem = pl.BlockSpec(memory_space=pltpu.SMEM)
    vmem = pl.BlockSpec(memory_space=pltpu.VMEM)
    depth = sub_count * picked[0].shape[1]
    versions = (lag_rows % 2 + 2 * away) * width

    def products(hops, dtype, name):
        flops = 2 * CAP * len(hops) * versions * width * depth
        return pl.pallas_call(
            functools.partial(lag_kernel, hops, lag_rows, away, block_count),
            out_shape=[jax.ShapeDtypeStruct((lag_rows, CAP, width, width), dtype)] * len(hops),
            in_specs=[smem, smem] + [vmem] * (1 + len(blocks)),
            out_specs=[vmem] * len(hops),
            scratch_shapes=[
                pltpu.VMEM((sub_count, width, depth // sub_count), BF16),
                pltpu.VMEM((sub_count, width, depth // sub_count), BF16),
                pltpu.VMEM((width, depth), BF16),
                pltpu.VMEM((versions, depth), BF16),
            ],
            compiler_params=pltpu.CompilerParams(vmem_limit_bytes=VMEM_LIMIT),
            cost_estimate=pl.CostEstimate(
                flops=flops, bytes_accessed=2 * REACH * width * depth, transcendentals=0
            ),
            name=name,
        )(pair_sides, pair_owner, table, *blocks)

    hops = tuple(range(1, hr_count))
    sent = products(hops, BF16, "lags_to_send")
    received = []
    for hop, part in zip(hops, sent):
        to_device = [(hr, (hr + hop) % hr_count) for hr in range(hr_count)]
        received.append(lax.ppermute(part, "hr", to_device))
    (summed,) = products((0,), F32, "lags_to_keep")
    for part in received:
        summed = summed + part.astype(F32)
    return (summed * norming).astype(BF16)


def solution(mesh):
    placed = (P(("grp", "hr"), "sub", None, "sta"), P(), P(), P("sta", None))
    return jax.shard_map(
        on_device,
        mesh=mesh,
        in_specs=placed,
        out_specs=P(("grp", "hr", "sub"), "sta", None, None),
        check_vma=False,
    )
```

time: 259 us -> 53 us (0.20)
  other arithmetic: 95 us -> 0.87 us
  local copies, waits for them, and re-layouts: 55.5 us -> 3.6 us
  waiting for transfers between devices: 60.6 us -> 31.5 us
  matrix products: 18.4 us -> 0 us
  between operations: 13.5 us -> 0.04 us
  loops' own time: 9.07 us -> 0 us
  Pallas kernels: 0 us -> 7.99 us
    another operation x32 -> x0, other arithmetic: 70.5 us -> none
    reduce_scatter x1 -> x0, waiting for transfers between devices: 37.2 us -> none  [on_device(): lax.psum_scatter(lag_term(jnp.int32(0), lag_rows * lax.axis_size(('hr', '...]
    ppermute x0 -> x8, waiting for transfers between devices: none -> 31.5 us  [the longest x3 21.3 us: on_device(): arrived.append(lax.ppermute(picked[reach], 'sta', to_owner))]
    all_to_all x1 -> x0, waiting for transfers between devices: 23.4 us -> none  [on_device(): lax.all_to_all(outgoing, 'sta', split_axis=0, concat_axis=0, tiled=True)]
    dot_general x16 -> x0, matrix products: 18.4 us -> none  [one_lag(): jnp.einsum('ski,skj->sij', turned, right_slots, preferred_element_type=jn...]
    gather x6 -> x0, local copies, waits for them, and re-layouts: 17.6 us -> none  [the longest x1 12.6 us: on_device(): picked = jnp.take(whitened, block_members.reshape(-1), axis=3)]
    reduce_sum x5 -> x0, other arithmetic: 9.63 us -> none  [the longest x2 9.21 us: whiten(): band_power = jnp.mean(banded * banded, axis=(2, 3), keepdims=True)]
    another operation x1 -> x0, loops' own time: 9.07 us -> none  [lag_term(): return lax.map(one_lag, jnp.arange(row_count, dtype=jnp.int32))]
  transfers between devices with their start and end apart: 2 -> 8, of which waited for: 2 -> 5; matrix products, arithmetic and copies ran while one was open for 1% -> 0% of each run, Pallas kernels for 0% -> 2%
where the time goes in v1:
time: 53 us; the launch traced here: 52.1 us
  waiting for transfers between devices  31.5 us (59%)
  starting transfers between devices  8.19 us (15%)
  Pallas kernels  7.99 us (15%)
  local copies, waits for them, and re-layouts  3.6 us (7%)
  other arithmetic  0.87 us (2%)
    ppermute x3, waiting for transfers between devices, on_device(): arrived.append(lax.ppermute(picked[reach], 'sta', to_owner))  21.3 us
    ppermute x1, waiting for transfers between devices, on_device(): received.append(lax.ppermute(part, 'hr', to_device))  8.76 us
    pallas_call x1, Pallas kernels, pick_blocks(): pl.pallas_call(functools.partial(pick_kernel, 'sta'), out_shape=[jax.Shap...  6.2 us
    ppermute x3, starting transfers between devices, on_device(): arrived.append(lax.ppermute(picked[reach], 'sta', to_owner))  6.12 us
    unnamed x10, local copies, waits for them, and re-layouts  3.6 us
    pallas_call x2, Pallas kernels, products(): pl.pallas_call(functools.partial(lag_kernel, hops, lag_rows, away, block_...  1.79 us
    ppermute x1, starting transfers between devices, on_device(): received.append(lax.ppermute(part, 'hr', to_device))  1.56 us
    ppermute x4, waiting for transfers between devices, on_device(): blocks.append(lax.ppermute(block, 'sub', swap))  1.39 us
  transfers between devices with their start and end apart: 8, of which 5 were waited for; matrix products, arithmetic and copies ran while one was open for 0% of the time, Pallas kernels for 2%

profile of v1, /device:TPU:0, one launch (start us, length us, event | category | flops | bytes accessed | tf_op | source)
XLA Modules:
  0.0 52.1 jit_solution(14576732312191735844)
XLA Ops:
  0.0 1.6 %copy-done = bf16[1,500,2,1024]{3,2,1,0:T(2,128)(2,1)S(1)} copy-done((bf16[1,500,2,1024]{3,2,1,0:T(2,128)(2,1)S(1)}, bf16[1,500,2,1024]{3,2,1,0:T(2,128)(2,1)}, u32[]{:S(2)}) %copy-start) | copy-done | bytes 2048024
  1.6 0.7 %copy-done.1 = s32[8,128]{1,0:T(8,128)S(1)} copy-done((s32[8,128]{1,0:T(8,128)S(1)}, s32[8,128]{1,0:T(8,128)}, u32[]{:S(2)}) %copy-start.1) | copy-done | bytes 4120
  2.3 0.7 %copy-done.2 = s32[4,2]{0,1:T(2,128)S(1)} copy-done((s32[4,2]{0,1:T(2,128)S(1)}, s32[4,2]{0,1:T(2,128)}, u32[]{:S(2)}) %copy-start.2) | copy-done | bytes 56
  2.9 0.7 %copy-done.3 = s32[4]{0:T(128)S(1)} copy-done((s32[4]{0:T(128)S(1)}, s32[4]{0:T(128)}, u32[]{:S(2)}) %copy-start.3) | copy-done | bytes 40
  3.6 6.2 %pick_and_whiten.1 = (bf16[128,1024]{1,0:T(8,128)(2,1)S(1)}, bf16[128,1024]{1,0:T(8,128)(2,1)S(1)}, bf16[128,1024]{1,0:T(8,128)(2,1)S(1)}, bf16[128,1024]{1,0:T(8,128)(2,1)S(1)}) custom-call(s32[2,4]{1,0:T(2,128)S(1)} %bitcast.1, s32[4]{0:T(128)S(1)} %copy-done.3, s32[8,128]{1,0:T(8,128)S(1)} %copy-done.1, bf16[1,500,2,1024]{3,2,1,0:T(2,128)(2,1)S(1)} %copy-done), custom_call_target="tpu_custom_call" | custom-call | flops 1048576000 | bytes 3096576 | tf_op jit(solution)/shard_map/pick_and_whiten/pallas_call | solution.py:137
  9.8 5.1 %collective-permute-start.1 = (bf16[128,1024]{1,0:T(8,128)(2,1)S(1)}, bf16[128,1024]{1,0:T(8,128)(2,1)S(1)}, u32[]{:S(2)}, u32[]{:S(2)}) collective-permute-start(bf16[128,1024]{1,0:T(8,128)(2,1)S(1)} %get-tuple-element.10), channel_id=1, source_target_pairs={{0,12},{4,0},{8,4},{12,8},{1,13},{5,1},{9,5},{13,9},{2,14},{6,2},{... | collective-permute-start | bytes 786440 | tf_op jit(solution)/shard_map/ppermute | solution.py:283
  14.9 0.0 collective-permute-start.3
  14.9 1.0 %collective-permute-start.5 = (bf16[128,1024]{1,0:T(8,128)(2,1)S(1)}, bf16[128,1024]{1,0:T(8,128)(2,1)S(1)}, u32[]{:S(2)}, u32[]{:S(2)}) collective-permute-start(bf16[128,1024]{1,0:T(8,128)(2,1)S(1)} %get-tuple-element.12), channel_id=1, source_target_pairs={{0,4},{4,8},{8,12},{12,0},{1,5},{5,9},{9,13},{13,1},{2,6},{6,10},{... | collective-permute-start | bytes 786440 | tf_op jit(solution)/shard_map/ppermute | solution.py:283
  15.9 0.0 collective-permute-start
  15.9 5.7 %collective-permute-done.1.rest_2_ = bf16[128,1024]{1,0:T(8,128)(2,1)S(1)} collective-permute-done((bf16[128,1024]{1,0:T(8,128)(2,1)S(1)}, bf16[128,1024]{1,0:T(8,128)(2,1)S(1)}, u32[]{:S(2)}, u32[]{:S(2)}) %collective-permute-start.1) | collective-permute-done | bytes 262176 | tf_op jit(solution)/shard_map/ppermute | solution.py:283
  21.7 0.0 collective-permute-start.2
  21.7 15.5 %collective-permute-done.3.rest_4_ = bf16[128,1024]{1,0:T(8,128)(2,1)S(1)} collective-permute-done((bf16[128,1024]{1,0:T(8,128)(2,1)S(1)}, bf16[128,1024]{1,0:T(8,128)(2,1)S(1)}, u32[]{:S(2)}, u32[]{:S(2)}) %collective-permute-start.3) | collective-permute-done | bytes 262176 | tf_op jit(solution)/shard_map/ppermute | solution.py:283
  37.2 0.0 collective-permute-start.4
  37.2 0.0 collective-permute-done.5.rest_6_
  37.2 0.5 collective-permute-start.6
  37.7 0.0 collective-permute-done.rest_1_
  37.7 0.0 collective-permute-done.2.rest_3_
  37.7 1.0 %collective-permute-done.4.rest_5_ = bf16[128,1024]{1,0:T(8,128)(2,1)S(1)} collective-permute-done((bf16[128,1024]{1,0:T(8,128)(2,1)S(1)}, bf16[128,1024]{1,0:T(8,128)(2,1)S(1)}, u32[]{:S(2)}, u32[]{:S(2)}) %collective-permute-start.4) | collective-permute-done | bytes 262176 | tf_op jit(solution)/shard_map/ppermute | solution.py:289
  38.8 0.4 collective-permute-done.6.rest_7_
  39.1 0.9 %lags_to_send.1 = bf16[4,3,128,128]{3,2,1,0:T(8,128)(2,1)S(1)} custom-call(s32[2,4]{1,0:T(2,128)S(1)} %bitcast.2, s32[4]{0:T(128)S(1)} %copy-done.3, f32[2,16,512]{2,1,0:T(8,128)S(1)} %copy-done.4, bf16[128,1024]{1,0:T(8,128)(2,1)S(1)} %get-tuple-element.9.rest_0_, bf16[128,1024]{1,0:T(8,128)(2,1)S(1)} %collective-permute-done.rest_1_, ...), custom_call_target="tpu_custom_call" | custom-call | flops 805306368 | bytes 2097152 | tf_op jit(solution)/shard_map/lags_to_send/pallas_call | solution.py:298
  40.0 1.6 %collective-permute-start.7 = (bf16[4,3,128,128]{3,2,1,0:T(8,128)(2,1)S(1)}, bf16[4,3,128,128]{3,2,1,0:T(8,128)(2,1)S(1)}, u32[]{:S(2)}, u32[]{:S(2)}) collective-permute-start(bf16[4,3,128,128]{3,2,1,0:T(8,128)(2,1)S(1)} %lags_to_send.1), channel_id=1, source_target_pairs={{0,2},{2,0},{1,3},{3,1},{4,6},{6,4},{5,7},{7,5},{8,10},{10,8},{9,1... | collective-permute-start | bytes 1179656 | tf_op jit(solution)/shard_map/ppermute | solution.py:321
  41.6 0.9 %lags_to_keep.1 = f32[4,3,128,128]{3,2,1,0:T(8,128)S(1)} custom-call(s32[2,4]{1,0:T(2,128)S(1)} %bitcast.3, s32[4]{0:T(128)S(1)} %copy-done.3, f32[2,16,512]{2,1,0:T(8,128)S(1)} %copy-done.4, bf16[128,1024]{1,0:T(8,128)(2,1)S(1)} %get-tuple-element.9.rest_0_, bf16[128,1024]{1,0:T(8,128)(2,1)S(1)} %collective-permute-done.rest_1_, ...), custom_call_target="tpu_custom_call" | custom-call | flops 805306368 | bytes 2097152 | tf_op jit(solution)/shard_map/lags_to_keep/pallas_call | solution.py:298
  42.5 8.8 %collective-permute-done.7 = bf16[4,3,128,128]{3,2,1,0:T(8,128)(2,1)S(1)} collective-permute-done((bf16[4,3,128,128]{3,2,1,0:T(8,128)(2,1)S(1)}, bf16[4,3,128,128]{3,2,1,0:T(8,128)(2,1)S(1)}, u32[]{:S(2)}, u32[]{:S(2)}) %collective-permute-start.7) | collective-permute-done | bytes 393248 | tf_op jit(solution)/shard_map/ppermute | solution.py:321
  51.3 0.9 %multiply_convert_fusion = bf16[4,3,128,128]{3,2,1,0:T(8,128)(2,1)} fusion(f32[4,3,128,128]{3,2,1,0:T(8,128)S(1)} %lags_to_keep.1, bf16[4,3,128,128]{3,2,1,0:T(8,128)(2,1)S(1)} %collective-permute-done.7), kind=kLoop, calls=%fused_computation | loop fusion | flops 786432 | bytes 1572864 | tf_op jit(solution)/shard_map/convert_element_type | solution.py:325
  (6 shorter events, 0.0 us)
Async XLA Ops:
  0.0 1.6 %copy-start = (bf16[1,500,2,1024]{3,2,1,0:T(2,128)(2,1)S(1)}, bf16[1,500,2,1024]{3,2,1,0:T(2,128)(2,1)}, u32[]{:S(2)}) copy-start(bf16[1,500,2,1024]{3,2,1,0:T(2,128)(2,1)} %x_ref.1) | copy-start | bytes 6144004
  1.6 0.7 %copy-start.1 = (s32[8,128]{1,0:T(8,128)S(1)}, s32[8,128]{1,0:T(8,128)}, u32[]{:S(2)}) copy-start(s32[8,128]{1,0:T(8,128)} %member_ref.1) | copy-start | bytes 12292
  2.3 0.7 %copy-start.2 = (s32[4,2]{0,1:T(2,128)S(1)}, s32[4,2]{0,1:T(2,128)}, u32[]{:S(2)}) copy-start(s32[4,2]{0,1:T(2,128)} %param.6) | copy-start | bytes 100
  2.9 0.7 %copy-start.3 = (s32[4]{0:T(128)S(1)}, s32[4]{0:T(128)}, u32[]{:S(2)}) copy-start(s32[4]{0:T(128)} %owner_ref.5) | copy-start | bytes 52
  3.6 35.5 %copy-start.4 = (f32[2,16,512]{2,1,0:T(8,128)S(1)}, f32[2,16,512]{2,1,0:T(8,128)}, u32[]{:S(2)}) copy-start(f32[2,16,512]{2,1,0:T(8,128)} %constant.4.clone.table_ref) | copy-start | bytes 196612
  9.8 11.9 %collective-permute-start.1 = (bf16[128,1024]{1,0:T(8,128)(2,1)S(1)}, bf16[128,1024]{1,0:T(8,128)(2,1)S(1)}, u32[]{:S(2)}, u32[]{:S(2)}) collective-permute-start(bf16[128,1024]{1,0:T(8,128)(2,1)S(1)} %get-tuple-element.10), channel_id=1, source_target_pairs={{0,12},{4,0},{8,4},{12,8},{1,13},{5,1},{9,5},{13,9},{2,14},{6,2},{... | collective-permute-start | bytes 786440 | tf_op jit(solution)/shard_map/ppermute | solution.py:283
  14.9 22.3 %collective-permute-start.3 = (bf16[128,1024]{1,0:T(8,128)(2,1)S(1)}, bf16[128,1024]{1,0:T(8,128)(2,1)S(1)}, u32[]{:S(2)}, u32[]{:S(2)}) collective-permute-start(bf16[128,1024]{1,0:T(8,128)(2,1)S(1)} %get-tuple-element.11), channel_id=1, source_target_pairs={{0,8},{4,12},{8,0},{12,4},{1,9},{5,13},{9,1},{13,5},{2,10},{6,14},... | collective-permute-start | bytes 786440 | tf_op jit(solution)/shard_map/ppermute | solution.py:283
  14.9 22.3 %collective-permute-start.5 = (bf16[128,1024]{1,0:T(8,128)(2,1)S(1)}, bf16[128,1024]{1,0:T(8,128)(2,1)S(1)}, u32[]{:S(2)}, u32[]{:S(2)}) collective-permute-start(bf16[128,1024]{1,0:T(8,128)(2,1)S(1)} %get-tuple-element.12), channel_id=1, source_target_pairs={{0,4},{4,8},{8,12},{12,0},{1,5},{5,9},{9,13},{13,1},{2,6},{6,10},{... | collective-permute-start | bytes 786440 | tf_op jit(solution)/shard_map/ppermute | solution.py:283
  15.9 21.8 %collective-permute-start = (bf16[128,1024]{1,0:T(8,128)(2,1)S(1)}, bf16[128,1024]{1,0:T(8,128)(2,1)S(1)}, u32[]{:S(2)}, u32[]{:S(2)}) collective-permute-start(bf16[128,1024]{1,0:T(8,128)(2,1)S(1)} %get-tuple-element.9.rest_0_), channel_id=1, source_target_pairs={{1,0},{0,1},{3,2},{2,3},{5,4},{4,5},{7,6},{6,7},{9,8},{8,9},{11,10... | collective-permute-start | bytes 786440 | tf_op jit(solution)/shard_map/ppermute | solution.py:289
  21.7 16.1 %collective-permute-start.2 = (bf16[128,1024]{1,0:T(8,128)(2,1)S(1)}, bf16[128,1024]{1,0:T(8,128)(2,1)S(1)}, u32[]{:S(2)}, u32[]{:S(2)}) collective-permute-start(bf16[128,1024]{1,0:T(8,128)(2,1)S(1)} %collective-permute-done.1.rest_2_), channel_id=1, source_target_pairs={{1,0},{0,1},{3,2},{2,3},{5,4},{4,5},{7,6},{6,7},{9,8},{8,9},{11,10... | collective-permute-start | bytes 786440 | tf_op jit(solution)/shard_map/ppermute | solution.py:289
  37.2 1.5 %collective-permute-start.4 = (bf16[128,1024]{1,0:T(8,128)(2,1)S(1)}, bf16[128,1024]{1,0:T(8,128)(2,1)S(1)}, u32[]{:S(2)}, u32[]{:S(2)}) collective-permute-start(bf16[128,1024]{1,0:T(8,128)(2,1)S(1)} %collective-permute-done.3.rest_4_), channel_id=1, source_target_pairs={{1,0},{0,1},{3,2},{2,3},{5,4},{4,5},{7,6},{6,7},{9,8},{8,9},{11,10... | collective-permute-start | bytes 786440 | tf_op jit(solution)/shard_map/ppermute | solution.py:289
  37.2 1.9 %collective-permute-start.6 = (bf16[128,1024]{1,0:T(8,128)(2,1)S(1)}, bf16[128,1024]{1,0:T(8,128)(2,1)S(1)}, u32[]{:S(2)}, u32[]{:S(2)}) collective-permute-start(bf16[128,1024]{1,0:T(8,128)(2,1)S(1)} %collective-permute-done.5.rest_6_), channel_id=1, source_target_pairs={{1,0},{0,1},{3,2},{2,3},{5,4},{4,5},{7,6},{6,7},{9,8},{8,9},{11,10... | collective-permute-start | bytes 786440 | tf_op jit(solution)/shard_map/ppermute | solution.py:289
  40.0 11.2 %collective-permute-start.7 = (bf16[4,3,128,128]{3,2,1,0:T(8,128)(2,1)S(1)}, bf16[4,3,128,128]{3,2,1,0:T(8,128)(2,1)S(1)}, u32[]{:S(2)}, u32[]{:S(2)}) collective-permute-start(bf16[4,3,128,128]{3,2,1,0:T(8,128)(2,1)S(1)} %lags_to_send.1), channel_id=1, source_target_pairs={{0,2},{2,0},{1,3},{3,1},{4,6},{6,4},{5,7},{7,5},{8,10},{10,8},{9,1... | collective-permute-start | bytes 1179656 | tf_op jit(solution)/shard_map/ppermute | solution.py:321
